TPU v7x, 32 devices: a whole 2x2x4 slice. The times are simulated.
32 devices in a mesh: rep: 2 (over x), dp: 16 (over z, y, core).
Axes of the slice: x: 2, y: 2, z: 4, core: 2. Of those that a mesh axis runs over, the one named last changes fastest.
Arguments:
- tokens: bfloat16 [32, 256, 2048], P(('rep', 'dp')), may hold values from -6 to 6
- cotangent: bfloat16 [32, 256, 2048], P(('rep', 'dp')), may hold values from -6 to 6
- branch: int32 [32, 2], P(('rep', 'dp')), may hold values from 32 to 128, as said below
- att_master: float32 [2048, 8192], P('dp')
- att_first: float32 [2, 2048, 8192], P('rep', 'dp')
- att_second: float32 [2, 2048, 8192], P('rep', 'dp')
- att_outer: float32 [2048, 8192], P('dp'), may hold values from -0.3125 to 0.3125
- mlp_master: float32 [2048, 24576], P('dp')
- mlp_first: float32 [2, 2048, 24576], P('rep', 'dp')
- mlp_second: float32 [2, 2048, 24576], P('rep', 'dp')
- mlp_outer: float32 [2048, 24576], P('dp'), may hold values from -0.3125 to 0.3125
Outputs:
- out_tokens: bfloat16 [32, 256, 2048], P(('rep', 'dp'))
- grad_tokens: float32 [32, 256, 2048], P(('rep', 'dp'))
- att_new: float32 [2048, 8192], P('dp')
- att_first_new: float32 [2, 2048, 8192], P('rep', 'dp')
- att_second_new: float32 [2, 2048, 8192], P('rep', 'dp')
- att_mean_diff: float32 [2048, 8192], P('dp')
- att_outer_new: float32 [2048, 8192], P('dp')
- mlp_new: float32 [2048, 24576], P('dp')
- mlp_first_new: float32 [2, 2048, 24576], P('rep', 'dp')
- mlp_second_new: float32 [2, 2048, 24576], P('rep', 'dp')
- mlp_mean_diff: float32 [2048, 24576], P('dp')
- mlp_outer_new: float32 [2048, 24576], P('dp')
Inputs may be any that keep to these rules, and one draw needn't show every extreme that they name: Continuation c of a unit follows the first branch[unit, c] prompt tokens; the value 128 occurs in every draw.
All inputs are finite; a program needn't handle non-finite values.
Results may differ from a plain program's by a relative error of at most 0.015.
Values may be sent and summed in bfloat16 or wider, within the bound.
A program may use at most 960 MiB of HBM per device.

v0:
```python
import math

import jax
import jax.numpy as jnp
from jax import lax
from jax.sharding import PartitionSpec as P

HEAD_DIM = 128
PROMPT = 128
CLEN = 64
CONT = 2
STEP = 10


LN_EPS = 1e-05
BETA_ONE = 0.9
BETA_TWO = 0.95
ADAM_EPS = 1e-08
DECAY = 0.1
RATE = 0.05
OUTER_RATE = 0.7
OUTER_MOMENTUM = 0.9
CONTRACT_LAST = (((1,), (1,)), ((), ()))
CONTRACT_FIRST = (((0,), (0,)), ((), ()))


def normalize(values):
    centre = values - jnp.mean(values, axis=-1, keepdims=True)
    factor = lax.rsqrt(jnp.mean(centre * centre, axis=-1, keepdims=True) + LN_EPS)
    return (centre * factor, factor)


def normalize_back(values, gradient):
    normed, factor = normalize(values)
    projection = jnp.mean(gradient * normed, axis=-1, keepdims=True)
    return factor * (gradient - jnp.mean(gradient, axis=-1, keepdims=True) - normed * projection)


def token_layout(seen, length):
    places = jnp.arange(length, dtype=jnp.int32)
    segment = jnp.where(places < PROMPT, -1, (places - PROMPT) // CLEN)
    within = jnp.where(places < PROMPT, places, (places - PROMPT) % CLEN)
    lookup = jnp.arange(CONT, dtype=jnp.int32)
    reach = jnp.sum(jnp.where(segment[:, None] == lookup[None, :], seen[None, :], 0), axis=1)
    position = jnp.where(segment < 0, places, reach + within)
    allowed = (segment[:, None] == segment[None, :]) & (within[None, :] <= within[:, None]) | (
        segment[None, :] < 0
    ) & (segment[:, None] >= 0) & (places[None, :] < reach[:, None])
    return (position, allowed)


def rotary_tables(position, depth):
    half_depth = depth // 2
    freqs = jnp.exp(jnp.arange(half_depth, dtype=jnp.float32) * (-2.0 * math.log(10000.0) / depth))
    angle = position.astype(jnp.float32)[:, None] * freqs[None, :]
    return (jnp.cos(angle)[:, None, :], jnp.sin(angle)[:, None, :])


def rotate(values, cosine, sine):
    half_depth = values.shape[-1] // 2
    first = values[..., :half_depth]
    second = values[..., half_depth:]
    return jnp.concatenate(
        [first * cosine - second * sine, second * cosine + first * sine], axis=-1
    )


def rotate_back(gradient, cosine, sine):
    half_depth = gradient.shape[-1] // 2
    first = gradient[..., :half_depth]
    second = gradient[..., half_depth:]
    return jnp.concatenate(
        [first * cosine + second * sine, second * cosine - first * sine], axis=-1
    )


def attention_scores(query, keys, allowed):
    scores = jnp.einsum(
        "qhd,khd->hqk", query, keys, preferred_element_type=jnp.float32
    ) * query.shape[-1] ** (-0.5)
    return jnp.where(allowed[None], scores, -1e30)


def adam_step(master, gradient, first, second):
    first_new = BETA_ONE * first + (1.0 - BETA_ONE) * gradient
    second_new = BETA_TWO * second + (1.0 - BETA_TWO) * gradient * gradient
    ratio = (
        first_new
        / (1.0 - BETA_ONE**STEP)
        / (jnp.sqrt(second_new / (1.0 - BETA_TWO**STEP)) + ADAM_EPS)
    )
    return (master - RATE * (ratio + DECAY * master), first_new, second_new)


def outer_step(master, mean_diff, momentum):
    momentum_new = OUTER_MOMENTUM * momentum + mean_diff
    return (master - OUTER_RATE * (mean_diff + OUTER_MOMENTUM * momentum_new), momentum_new)


def on_device(
    tokens,
    cotangent,
    branch,
    att_master,
    att_first,
    att_second,
    att_outer,
    mlp_master,
    mlp_first,
    mlp_second,
    mlp_outer,
):
    units, length, width = tokens.shape
    hidden_width = mlp_master.shape[1] // 3
    depth = HEAD_DIM
    heads = width // depth
    count = units * length
    flat = tokens.reshape(count, width).astype(jnp.float32)
    att_low = att_master.astype(jnp.bfloat16)
    mlp_low = mlp_master.astype(jnp.bfloat16)
    gate_part = mlp_low[:, : 2 * hidden_width]
    down_part = mlp_low[:, 2 * hidden_width :]
    att_full = lax.all_gather(att_low, "dp", axis=0, tiled=True)
    normed_one = normalize(flat)[0].astype(jnp.bfloat16)
    projected = jnp.dot(normed_one, att_full[:, : 3 * width], preferred_element_type=jnp.float32)
    projected = projected.reshape(units, length, 3, heads, depth)

    def attend(inputs):
        block, seen = inputs
        position, allowed = token_layout(seen, length)
        cosine, sine = rotary_tables(position, depth)
        query = rotate(block[:, 0], cosine, sine).astype(jnp.bfloat16)
        keys = rotate(block[:, 1], cosine, sine).astype(jnp.bfloat16)
        values = block[:, 2].astype(jnp.bfloat16)
        scores = attention_scores(query, keys, allowed)
        highest = jnp.max(scores, axis=-1, keepdims=True)
        powers = jnp.exp(scores - highest)
        totals = jnp.sum(powers, axis=-1, keepdims=True)
        weights = (powers / totals).astype(jnp.bfloat16)
        mixed_unit = jnp.einsum("hqk,khd->qhd", weights, values, preferred_element_type=jnp.float32)
        return (
            query,
            keys,
            values,
            (highest + jnp.log(totals))[..., 0],
            mixed_unit.astype(jnp.bfloat16),
        )

    query_all, key_all, value_all, log_totals, mixed = lax.map(attend, (projected, branch))
    mixed_flat = mixed.reshape(count, width)
    attended = lax.dot_general(
        mixed_flat, att_full[:, 3 * width :], CONTRACT_LAST, preferred_element_type=jnp.float32
    )
    resid = flat + attended
    normed_two = normalize(resid)[0].astype(jnp.bfloat16)
    gate_full, down_full = (
        lax.all_gather(gate_part, "dp", axis=0, tiled=True),
        lax.all_gather(down_part, "dp", axis=0, tiled=True),
    )
    gate_up = jnp.dot(normed_two, gate_full, preferred_element_type=jnp.float32)
    gate_value = gate_up[:, :hidden_width]
    up_value = gate_up[:, hidden_width:]
    sigmoid_gate = jax.nn.sigmoid(gate_value)
    silu_gate = gate_value * sigmoid_gate
    hidden = (silu_gate * up_value).astype(jnp.bfloat16)
    fed = lax.dot_general(hidden, down_full, CONTRACT_LAST, preferred_element_type=jnp.float32)
    out_tokens = (resid + fed).astype(jnp.bfloat16).reshape(units, length, width)
    att_back, gate_back, down_back = (
        lax.all_gather(att_low, "dp", axis=0, tiled=True),
        lax.all_gather(gate_part, "dp", axis=0, tiled=True),
        lax.all_gather(down_part, "dp", axis=0, tiled=True),
    )
    grad_fed = cotangent.reshape(count, width)
    grad_out = grad_fed.astype(jnp.float32)
    grad_hidden = jnp.dot(grad_fed, down_back, preferred_element_type=jnp.float32)
    grad_gate = grad_hidden * up_value * sigmoid_gate * (1.0 + gate_value * (1.0 - sigmoid_gate))
    grad_up = grad_hidden * silu_gate
    grad_gate_up = jnp.concatenate([grad_gate, grad_up], axis=1).astype(jnp.bfloat16)
    grad_normed_two = lax.dot_general(
        grad_gate_up, gate_back, CONTRACT_LAST, preferred_element_type=jnp.float32
    )
    grad_resid = grad_out + normalize_back(resid, grad_normed_two)
    grad_attended = grad_resid.astype(jnp.bfloat16)
    grad_mixed = jnp.dot(
        grad_attended, att_back[:, 3 * width :], preferred_element_type=jnp.float32
    )
    grad_mixed = grad_mixed.astype(jnp.bfloat16).reshape(units, length, heads, depth)

    def attend_back(inputs):
        query, keys, values, log_total, grad_unit, seen = inputs
        position, allowed = token_layout(seen, length)
        cosine, sine = rotary_tables(position, depth)
        scores = attention_scores(query, keys, allowed)
        weights = jnp.exp(scores - log_total[..., None])
        grad_weights = jnp.einsum(
            "qhd,khd->hqk", grad_unit, values, preferred_element_type=jnp.float32
        )
        grad_values = jnp.einsum(
            "hqk,qhd->khd",
            weights.astype(jnp.bfloat16),
            grad_unit,
            preferred_element_type=jnp.float32,
        )
        grad_scores = weights * (
            grad_weights - jnp.sum(grad_weights * weights, axis=-1, keepdims=True)
        )
        grad_scores = grad_scores.astype(jnp.bfloat16)
        scale = depth ** (-0.5)
        grad_query = (
            jnp.einsum("hqk,khd->qhd", grad_scores, keys, preferred_element_type=jnp.float32)
            * scale
        )
        grad_keys = (
            jnp.einsum("hqk,qhd->khd", grad_scores, query, preferred_element_type=jnp.float32)
            * scale
        )
        grad_query = rotate_back(grad_query, cosine, sine)
        grad_keys = rotate_back(grad_keys, cosine, sine)
        return jnp.stack([grad_query, grad_keys, grad_values], axis=1).astype(jnp.bfloat16)

    grad_projected = lax.map(
        attend_back, (query_all, key_all, value_all, log_totals, grad_mixed, branch)
    )
    grad_projected = grad_projected.reshape(count, 3 * width)
    grad_normed_one = lax.dot_general(
        grad_projected, att_back[:, : 3 * width], CONTRACT_LAST, preferred_element_type=jnp.float32
    )
    grad_tokens = (grad_resid + normalize_back(flat, grad_normed_one)).reshape(units, length, width)
    left_inputs = normed_one
    left_grads = grad_attended
    first_block = lax.dot_general(
        left_inputs, grad_projected, CONTRACT_FIRST, preferred_element_type=jnp.float32
    )
    second_block = lax.dot_general(
        left_grads, mixed_flat, CONTRACT_FIRST, preferred_element_type=jnp.float32
    )
    att_grad = lax.psum_scatter(
        jnp.concatenate([first_block, second_block], axis=1), "dp", scatter_dimension=0, tiled=True
    )
    left_inputs = normed_two
    left_grads = grad_fed
    first_block = lax.dot_general(
        left_inputs, grad_gate_up, CONTRACT_FIRST, preferred_element_type=jnp.float32
    )
    second_block = lax.dot_general(
        left_grads, hidden, CONTRACT_FIRST, preferred_element_type=jnp.float32
    )
    mlp_grad = lax.psum_scatter(
        jnp.concatenate([first_block, second_block], axis=1), "dp", scatter_dimension=0, tiled=True
    )
    att_inner, att_one, att_two = adam_step(att_master, att_grad, att_first[0], att_second[0])
    mlp_inner, mlp_one, mlp_two = adam_step(mlp_master, mlp_grad, mlp_first[0], mlp_second[0])
    att_total, mlp_total = (
        lax.psum((att_master - att_inner).astype(jnp.bfloat16), "rep").astype(jnp.float32),
        lax.psum((mlp_master - mlp_inner).astype(jnp.bfloat16), "rep").astype(jnp.float32),
    )
    groups = lax.axis_size("rep")
    att_mean = att_total / groups
    mlp_mean = mlp_total / groups
    att_new, att_momentum = outer_step(att_master, att_mean, att_outer)
    mlp_new, mlp_momentum = outer_step(mlp_master, mlp_mean, mlp_outer)
    return (
        out_tokens,
        grad_tokens,
        att_new,
        att_one[None],
        att_two[None],
        att_mean,
        att_momentum,
        mlp_new,
        mlp_one[None],
        mlp_two[None],
        mlp_mean,
        mlp_momentum,
    )


def solution(mesh):
    in_specs = (
        P(("rep", "dp"), None, None),
        P(("rep", "dp"), None, None),
        P(("rep", "dp"), None),
        P("dp", None),
        P("rep", "dp", None),
        P("rep", "dp", None),
        P("dp", None),
        P("dp", None),
        P("rep", "dp", None),
        P("rep", "dp", None),
        P("dp", None),
    )
    out_specs = (
        P(("rep", "dp"), None, None),
        P(("rep", "dp"), None, None),
        P("dp", None),
        P("rep", "dp", None),
        P("rep", "dp", None),
        P("dp", None),
        P("dp", None),
        P("dp", None),
        P("rep", "dp", None),
        P("rep", "dp", None),
        P("dp", None),
        P("dp", None),
    )
    return jax.shard_map(
        on_device, mesh=mesh, in_specs=in_specs, out_specs=out_specs, check_vma=False
    )
```

profile of v0, /device:TPU:0, one launch (start us, length us, event | category | flops | bytes accessed | tf_op | source)
XLA Modules:
  0.0 3510.7 jit_solution(4351065255561334585)
XLA Ops:
  7.2 3.8 convert_element_type.109
  11.1 5.3 convert_element_type.116
  16.4 2.7 copy-done.2
  19.1 3.0 slice.91
  22.1 0.0 all-gather.8.cloned.1.call-start
  22.2 3.2 slice.94
  25.5 0.1 fusion.65
  25.6 0.2 convert_reduce_fusion
  25.9 0.4 fusion.35
  26.3 0.2 fusion.64
  26.5 0.3 multiply_cosine_fusion
  26.8 155.1 %all-gather.4.cloned.1.call-done = bf16[2048,8192]{1,0:T(8,128)(2,1)} async-done(((bf16[128,8192]{1,0:T(8,128)(2,1)}), bf16[2048,8192]{1,0:T(8,128)(2,1)}) %all-gather.4.cloned.1.call-update) | async-done | bytes 33554448 | tf_op jit(solution)/shard_map/all_gather | solution.py:123
  181.9 21.3 slice_bitcast_fusion
  203.2 32.2 copy.47
  235.4 12.6 fusion.50
  248.1 0.3 slice_bitcast_fusion.2
  248.4 0.7 subtract_convert_fusion.1
  249.1 1.4 copy-done.13
  250.5 0.9 fusion.82
  251.4 0.6 fusion.14
  252.0 0.9 fusion.46
  252.9 0.5 copy-done
  253.4 6.4 fusion.83
  259.8 0.3 multiply_reduce_fusion.2
  260.2 250.0 %all-gather.6.cloned.1.call-done = bf16[2048,16384]{1,0:T(8,128)(2,1)} async-done(((bf16[128,16384]{1,0:T(8,128)(2,1)}), bf16[2048,16384]{1,0:T(8,128)(2,1)}) %all-gather.6.cloned.1.call-update) | async-done | bytes 67108880 | tf_op jit(solution)/shard_map/all_gather | solution.py:157
  510.2 33.9 fusion.78
  544.1 136.4 %all-gather.8.cloned.1.call-done = bf16[2048,8192]{1,0:T(8,128)(2,1)} async-done(((bf16[128,8192]{1,0:T(8,128)(2,1)}), bf16[2048,8192]{1,0:T(8,128)(2,1)}) %all-gather.8.cloned.1.call-update) | async-done | bytes 33554448 | tf_op jit(solution)/shard_map/all_gather | solution.py:158
  680.5 24.6 multiply_convert_fusion.1
  705.1 29.3 fusion.81
  734.5 3.3 multiply_add_fusion.2
  737.8 7.4 fusion.22
  745.2 2.3 copy.69
  747.5 4.3 multiply_reduce_fusion
  751.8 0.3 copy-done.9
  752.1 0.9 fusion.42
  753.0 1.0 multiply_convert_fusion.3
  754.0 0.1 copy-done.20
  754.2 0.8 multiply_bitcast_fusion
  755.0 0.2 copy-done.14
  755.2 0.2 copy-done.16
  755.4 0.5 multiply_bitcast_fusion.1
  755.9 8.2 fusion.57
  764.0 0.7 multiply_add_fusion.4
  764.8 0.1 maximum_bitcast_fusion
  764.9 0.1 maximum_bitcast_fusion.1
  765.0 2.0 maximum_convert_fusion
  767.0 21.6 fusion.55
  788.6 43.4 %pad_maximum_fusion.1 = f32[2048,8192]{1,0:T(8,128)} fusion(f32[2048,2048]{1,0:T(8,128)} %fusion.57, f32[2048,6144]{1,0:T(8,128)} %fusion.55), kind=kLoop, calls=%fused_computation.1 | loop fusion | flops 16777216 | bytes 134217728 | tf_op jit(solution)/shard_map/concatenate | solution.py:238
  832.0 0.0 reduce-scatter.7.cloned.1.call-start
  832.0 1.1 copy-done.12
  833.2 39.6 %convolution_bitcast_fusion = f32[2048,8192]{1,0:T(8,128)} fusion(bf16[256,8192]{1,0:T(8,128)(2,1)} %get-tuple-element.77, bf16[1,256,2048]{2,1,0:T(8,128)(2,1)S(1)} %copy-done.12), kind=kOutput, calls=%fused_computation.2 | convolution fusion | flops 8589934592 | bytes 72351744 | tf_op jit(solution)/shard_map/dot_general | solution.py:245
  872.8 69.0 %fusion.9 = f32[2048,16384]{1,0:T(8,128)} fusion(bf16[256,8192]{1,0:T(8,128)(2,1)} %get-tuple-element.76, bf16[256,8192]{1,0:T(8,128)(2,1)} %get-tuple-element.75, f32[256,2048]{1,0:T(8,128)S(1)} %copy-done.8, f32[256]{0:T(256)S(1)} %add_rsqrt_fusion, f32[256]{0:T(256)S(1)} %broadcast_multiply_fusion.4), kind=kOutput, calls=%fused_computation.27 | convolution fusion | flops 17198219264 | bytes 144705536 | tf_op jit(solution)/shard_map/dot_general | solution.py:242
  941.8 134.1 %pad_maximum_fusion = f32[2048,24576]{1,0:T(8,128)} fusion(f32[2048,8192]{1,0:T(8,128)} %convolution_bitcast_fusion, f32[2048,16384]{1,0:T(8,128)} %fusion.9), kind=kLoop, calls=%fused_computation | loop fusion | flops 50331648 | bytes 402653184 | tf_op jit(solution)/shard_map/concatenate | solution.py:249
  1076.0 393.2 %reduce-scatter.5.cloned.1.call-done = f32[128,8192]{1,0:T(8,128)} async-done(((f32[2048,8192]{1,0:T(8,128)}), f32[128,8192]{1,0:T(8,128)}) %reduce-scatter.5.cloned.1.call-update) | async-done | bytes 4194320 | tf_op jit(solution)/shard_map/reduce_scatter | solution.py:237
  1469.1 11.0 fusion.48
  1480.1 1761.1 %reduce-scatter.7.cloned.1.call-done = f32[128,24576]{1,0:T(8,128)} async-done(((f32[2048,24576]{1,0:T(8,128)}), f32[128,24576]{1,0:T(8,128)}) %reduce-scatter.7.cloned.1.call-update) | async-done | bytes 12582928
  3241.2 32.9 fusion.15
  3274.1 1.2 copy-done.6
  3275.3 14.6 fusion.80
  3289.9 3.7 fusion.34
  3293.6 18.3 fusion.27
  3311.9 160.0 %all-reduce.4.cloned.1.call-done = (bf16[128,8192]{1,0:T(8,128)(2,1)}, bf16[128,24576]{1,0:T(8,128)(2,1)}) async-done(((bf16[128,8192]{1,0:T(8,128)(2,1)}, bf16[128,24576]{1,0:T(8,128)(2,1)}), (bf16[128,8192]{1,0:T(8,128)(2,1)}, bf16[128,24576]{1,0:T(8,128)(2,1)})) %all-reduce.4.cloned.1.call-update) | async-done | bytes 8388624 | tf_op jit(solution)/shard_map/psum | solution.py:254
  3472.0 10.2 multiply_subtract_fusion.1
  3482.1 21.3 multiply_subtract_fusion
  (70 shorter events, 0.5 us)
Async XLA Ops:
  7.2 174.7 %all-gather.4.cloned.1.call-start = ((), (), s32[]{:S(2)}) async-start(), calls=%async_computation.2 | async-start | bytes 35651584 | tf_op jit(solution)/shard_map/all_gather | solution.py:123
  11.0 499.2 %all-gather.6.cloned.1.call-start = ((), (), s32[]{:S(2)}) async-start(), calls=%async_computation.3 | async-start | bytes 71303168 | tf_op jit(solution)/shard_map/all_gather | solution.py:157
  16.4 2.7 copy-start.2
  22.1 3.4 copy-start.27
  22.1 3.5 copy-start.5
  22.1 658.4 %all-gather.8.cloned.1.call-start = ((), (), s32[]{:S(2)}) async-start(), calls=%async_computation.4 | async-start | bytes 35651584 | tf_op jit(solution)/shard_map/all_gather | solution.py:158
  25.4 1443.7 %reduce-scatter.5.cloned.1.call-start = ((), (), s32[]{:S(2)}) async-start(), calls=%async_computation.5 | async-start | bytes 71303168 | tf_op jit(solution)/shard_map/reduce_scatter | solution.py:237
  25.8 741.1 %copy-start.23 = (f32[256]{0:T(256)}, f32[256]{0:T(256)S(1)}, u32[]{:S(2)}) copy-start(f32[256]{0:T(256)S(1)} %broadcast_multiply_fusion.5) | copy-start | bytes 3076
  26.3 740.7 %copy-start.25 = (f32[256]{0:T(256)}, f32[256]{0:T(256)S(1)}, u32[]{:S(2)}) copy-start(f32[256]{0:T(256)S(1)} %add_rsqrt_fusion.1) | copy-start | bytes 3076
  248.1 3.9 copy-start.11
  249.1 1.4 copy-start.13
  249.1 2.3 copy-start.15
  249.1 2.3 copy-start.17
  249.1 2.9 copy-start.19
  251.4 2.0 copy-start
  253.4 6.4 copy-start.21
  259.8 445.3 %copy-start.7 = (f32[256,2048]{1,0:T(8,128)}, f32[256,2048]{1,0:T(8,128)S(1)}, u32[]{:S(2)}) copy-start(f32[256,2048]{1,0:T(8,128)S(1)} %get-tuple-element.100) | copy-start | bytes 6291460
  737.8 18.1 copy-start.3
  747.5 4.4 copy-start.1
  747.5 4.6 copy-start.9
  753.0 1.1 copy-start.18
  753.0 1.2 copy-start.20
  754.2 1.0 copy-start.14
  754.2 1.2 copy-start.16
  754.2 1.7 copy-start.22
  832.0 1.2 copy-start.12
  832.0 2409.2 %reduce-scatter.7.cloned.1.call-start = ((), (), s32[]{:S(2)}) async-start(), calls=%async_computation.6 | async-start | bytes 213909504
  833.2 39.6 %copy-start.8 = (f32[256,2048]{1,0:T(8,128)S(1)}, f32[256,2048]{1,0:T(8,128)}, u32[]{:S(2)}) copy-start(f32[256,2048]{1,0:T(8,128)} %copy-done.7) | copy-start | bytes 6291460
  1075.9 2396.0 %all-reduce.4.cloned.1.call-start = ((), (), s32[]{:S(2)}) async-start(), calls=%async_computation.7 | async-start | bytes 16777216 | tf_op jit(solution)/shard_map/psum | solution.py:254
  3274.0 1.2 copy-start.6
  3274.0 1.2 copy-start.24
  3274.0 1.2 copy-start.26
  3275.3 14.7 copy-start.4
  3472.0 10.2 copy-start.10
Sparse Core Ops, SparseCore 0:
  11.1 170.7 all-gather.3
  184.1 326.1 all-gather.5
  512.4 168.0 all-gather.7
  832.1 636.9 reduce-scatter.4
  1473.2 1767.9 reduce-scatter.6
  3274.2 197.7 all-reduce.3
where the time goes:
time: 3520 us; the launch traced here: 3510 us
  waiting for transfers between devices  2860 us (81%)
  matrix products  294 us (8%)
  other arithmetic  276 us (8%)
  local copies, waits for them, and re-layouts  70 us (2%)
    unnamed x7, waiting for transfers between devices  1760 us
    reduce_scatter x1, waiting for transfers between devices, on_device(): lax.psum_scatter(jnp.concatenate([first_block, second_block], axis=1), 'd...  393 us
    all_gather x1, waiting for transfers between devices, on_device(): lax.all_gather(gate_part, 'dp', axis=0, tiled=True)  250 us
    concatenate x2, other arithmetic, on_device(): jnp.concatenate([first_block, second_block], axis=1)  177 us
    psum x1, waiting for transfers between devices, on_device(): lax.psum((att_master - att_inner).astype(jnp.bfloat16), 'rep')  160 us
    all_gather x1, waiting for transfers between devices, on_device(): att_full = lax.all_gather(att_low, 'dp', axis=0, tiled=True)  155 us
    all_gather x1, waiting for transfers between devices, on_device(): lax.all_gather(down_part, 'dp', axis=0, tiled=True)  136 us
  transfers between devices with their start and end apart: 6, of which 6 were waited for; matrix products, arithmetic and copies ran while one was open for 12% of the time, Pallas kernels for 0%

commit v1 on v0

v1 whole, which is shorter than its diff:
```python
import math

import jax
import jax.numpy as jnp
from jax import lax
from jax.sharding import PartitionSpec as P

HEAD_DIM = 128
PROMPT = 128
CLEN = 64
CONT = 2
STEP = 10
TEAM = 8


LN_EPS = 1e-05
BETA_ONE = 0.9
BETA_TWO = 0.95
ADAM_EPS = 1e-08
DECAY = 0.1
RATE = 0.05
OUTER_RATE = 0.7
OUTER_MOMENTUM = 0.9
CONTRACT_LAST = (((1,), (1,)), ((), ()))
CONTRACT_FIRST = (((0,), (0,)), ((), ()))
LOW = jnp.bfloat16
FULL = jnp.float32


def normalize(values):
    centre = values - jnp.mean(values, axis=-1, keepdims=True)
    factor = lax.rsqrt(jnp.mean(centre * centre, axis=-1, keepdims=True) + LN_EPS)
    return (centre * factor, factor)


def normalize_back(values, gradient):
    normed, factor = normalize(values)
    projection = jnp.mean(gradient * normed, axis=-1, keepdims=True)
    return factor * (gradient - jnp.mean(gradient, axis=-1, keepdims=True) - normed * projection)


def token_layout(seen, length):
    places = jnp.arange(length, dtype=jnp.int32)
    segment = jnp.where(places < PROMPT, -1, (places - PROMPT) // CLEN)
    within = jnp.where(places < PROMPT, places, (places - PROMPT) % CLEN)
    lookup = jnp.arange(CONT, dtype=jnp.int32)
    reach = jnp.sum(jnp.where(segment[:, None] == lookup[None, :], seen[None, :], 0), axis=1)
    position = jnp.where(segment < 0, places, reach + within)
    allowed = (segment[:, None] == segment[None, :]) & (within[None, :] <= within[:, None]) | (
        segment[None, :] < 0
    ) & (segment[:, None] >= 0) & (places[None, :] < reach[:, None])
    return (position, allowed)


def rotary_tables(position, depth):
    half_depth = depth // 2
    freqs = jnp.exp(jnp.arange(half_depth, dtype=jnp.float32) * (-2.0 * math.log(10000.0) / depth))
    angle = position.astype(jnp.float32)[:, None] * freqs[None, :]
    return (jnp.cos(angle)[:, None, :], jnp.sin(angle)[:, None, :])


def rotate(values, cosine, sine):
    half_depth = values.shape[-1] // 2
    first = values[..., :half_depth]
    second = values[..., half_depth:]
    return jnp.concatenate(
        [first * cosine - second * sine, second * cosine + first * sine], axis=-1
    )


def rotate_back(gradient, cosine, sine):
    half_depth = gradient.shape[-1] // 2
    first = gradient[..., :half_depth]
    second = gradient[..., half_depth:]
    return jnp.concatenate(
        [first * cosine + second * sine, second * cosine - first * sine], axis=-1
    )


def adam_step(master, gradient, first, second):
    first_new = BETA_ONE * first + (1.0 - BETA_ONE) * gradient
    second_new = BETA_TWO * second + (1.0 - BETA_TWO) * gradient * gradient
    ratio = (
        first_new
        / (1.0 - BETA_ONE**STEP)
        / (jnp.sqrt(second_new / (1.0 - BETA_TWO**STEP)) + ADAM_EPS)
    )
    return (master - RATE * (ratio + DECAY * master), first_new, second_new)


def outer_step(master, mean_diff, momentum):
    momentum_new = OUTER_MOMENTUM * momentum + mean_diff
    return (master - OUTER_RATE * (mean_diff + OUTER_MOMENTUM * momentum_new), momentum_new)


def dot(left, right, dims=(((1,), (0,)), ((), ()))):
    return lax.dot_general(left, right, dims, preferred_element_type=FULL)


def on_device(
    reps,
    ranks,
    tokens,
    cotangent,
    branch,
    att_master,
    att_first,
    att_second,
    att_outer,
    mlp_master,
    mlp_first,
    mlp_second,
    mlp_outer,
):
    units, length, width = tokens.shape
    hidden_width = mlp_master.shape[1] // 3
    depth = HEAD_DIM
    count = units * length
    rows = att_master.shape[0]
    team = TEAM
    att_share = width // team
    hid_share = hidden_width // team
    me = lax.axis_index("dp")
    rep = lax.axis_index("rep")
    mate = me % team

    def hop(values, other):
        pairs = [(r * ranks + i, r * ranks + (i ^ other)) for r in range(reps) for i in range(ranks)]
        return lax.ppermute(values, ("rep", "dp"), pairs)

    def swap(values):
        pairs = [(r * ranks + i, (1 - r) * ranks + i) for r in range(reps) for i in range(ranks)]
        return lax.ppermute(values, ("rep", "dp"), pairs)

    def team_gather(block):
        half = block.shape[0] // 2
        core = hop(block, 1)
        second = hop(block, 2)
        third = hop(block, 4)
        both = jnp.concatenate([hop(third[:half], 2), hop(second[half:], 4)])
        return jnp.stack(
            [block, core, second, hop(second, 1), third, hop(third, 1), both, hop(both, 1)]
        )

    def team_sum(parts):
        half = parts.shape[1] // 2
        sent = hop(parts[1::2], 1)
        pair = parts[0::2].astype(FULL) + sent.astype(FULL)
        over_second = hop(pair[3, :half].astype(LOW), 2)
        over_third = hop(pair[3, half:].astype(LOW), 4)
        for_third = jnp.concatenate([pair[2, :half] + over_second, pair[2, half:]]).astype(LOW)
        for_second = jnp.concatenate([pair[1, :half], pair[1, half:] + over_third]).astype(LOW)
        return pair[0] + hop(for_second, 2).astype(FULL) + hop(for_third, 4).astype(FULL)

    def share_out(master, bases, share):
        low = master.astype(LOW)
        return jnp.concatenate(
            [
                low[:, base : base + team * share].reshape(rows, team, share).transpose(1, 0, 2)
                for base in bases
            ],
            axis=2,
        )

    def weight_gather(shares):
        total = shares.shape[2]
        result = jnp.zeros((ranks * rows, total), LOW)
        for other in range(ranks):
            block = lax.dynamic_index_in_dim(shares, (me ^ other) % team, 0, keepdims=False)
            start = (me ^ other) * rows
            if other < team or reps != 2:
                part = hop(block, other) if other else block
                result = lax.dynamic_update_slice(result, part, (start, 0))
            else:
                half = rows // 2
                part = hop(lax.dynamic_slice(block, (rep * half, 0), (half, total)), other)
                result = lax.dynamic_update_slice(result, part, (start + rep * half, 0))
                part = swap(part)
                result = lax.dynamic_update_slice(result, part, (start + (1 - rep) * half, 0))
        return result

    def grad_scatter(grad):
        sums = []
        for low_bits in range(team):
            total = None
            for high_bits in range(ranks // team):
                other = high_bits * team + low_bits
                block = lax.dynamic_slice(grad, ((me ^ other) * rows, 0), (rows, grad.shape[1]))
                block = (hop(block, other) if other else block).astype(FULL)
                total = block if total is None else total + block
            sums.append(total)
        return jnp.take(jnp.stack(sums), jnp.arange(team) ^ mate, axis=0)

    def spread(sums, pieces):
        share = sums.shape[2] // pieces
        return [
            sums[:, :, p * share : (p + 1) * share].transpose(1, 0, 2).reshape(rows, team * share)
            for p in range(pieces)
        ]

    flat = tokens.reshape(count, width).astype(FULL)
    grad_fed_own = cotangent.reshape(count, width)
    seen_all = jnp.stack([branch if k == 0 else hop(branch, k) for k in range(team)])
    seen_all = seen_all.reshape(team * units, CONT)
    normed_one = team_gather(normalize(flat)[0].astype(LOW)).reshape(team * count, width)
    att_low = weight_gather(
        share_out(att_master, [0, width, 2 * width, 3 * width], att_share)
    )
    qkv_low, out_low = att_low[:, : 3 * att_share], att_low[:, 3 * att_share :]
    gate_low = weight_gather(share_out(mlp_master, [0, hidden_width], hid_share))
    down_low = weight_gather(share_out(mlp_master, [2 * hidden_width], hid_share))
    grad_fed = team_gather(grad_fed_own).reshape(team * count, width)

    heads = att_share // depth
    position, allowed = jax.vmap(lambda seen: token_layout(seen, length))(seen_all)
    cosine, sine = jax.vmap(lambda places: rotary_tables(places, depth))(position)
    projected = dot(normed_one, qkv_low).reshape(team * units, length, 3, heads, depth)
    query = rotate(projected[:, :, 0], cosine, sine).astype(LOW)
    keys = rotate(projected[:, :, 1], cosine, sine).astype(LOW)
    values = projected[:, :, 2].astype(LOW)
    scale = depth ** (-0.5)

    def ein(spec, left, right):
        return jnp.einsum(spec, left, right, preferred_element_type=FULL)

    scores = jnp.where(allowed[:, None], ein("uqhd,ukhd->uhqk", query, keys) * scale, -1e30)
    highest = jnp.max(scores, axis=-1, keepdims=True)
    powers = jnp.exp(scores - highest)
    prob = powers / jnp.sum(powers, axis=-1, keepdims=True)
    prob_low = prob.astype(LOW)
    mixed = ein("uhqk,ukhd->uqhd", prob_low, values).astype(LOW).reshape(team * count, att_share)
    attended = dot(mixed, out_low, CONTRACT_LAST).astype(LOW).reshape(team, count, width)
    resid = flat + team_sum(attended)
    normed_two = team_gather(normalize(resid)[0].astype(LOW)).reshape(team * count, width)
    gate_up = dot(normed_two, gate_low)
    gate_value = gate_up[:, :hid_share]
    up_value = gate_up[:, hid_share:]
    sigmoid_gate = jax.nn.sigmoid(gate_value)
    silu_gate = gate_value * sigmoid_gate
    hidden = (silu_gate * up_value).astype(LOW)
    down_grad = grad_scatter(dot(grad_fed, hidden, CONTRACT_FIRST).astype(LOW))
    grad_hidden = dot(grad_fed, down_low)
    grad_gate = grad_hidden * up_value * sigmoid_gate * (1.0 + gate_value * (1.0 - sigmoid_gate))
    grad_up = grad_hidden * silu_gate
    grad_gate_up = jnp.concatenate([grad_gate, grad_up], axis=1).astype(LOW)
    gate_grad = grad_scatter(dot(normed_two, grad_gate_up, CONTRACT_FIRST).astype(LOW))
    grad_normed_two = dot(grad_gate_up, gate_low, CONTRACT_LAST).astype(LOW)
    grad_normed_two = team_sum(grad_normed_two.reshape(team, count, width))
    grad_resid = grad_fed_own.astype(FULL) + normalize_back(resid, grad_normed_two)
    grad_attended = team_gather(grad_resid.astype(LOW)).reshape(team * count, width)
    grad_mixed = dot(grad_attended, out_low).astype(LOW)
    out_grad = dot(grad_attended, mixed, CONTRACT_FIRST)
    grad_mixed = grad_mixed.reshape(team * units, length, heads, depth)
    grad_prob = ein("uqhd,ukhd->uhqk", grad_mixed, values)
    grad_values = ein("uhqk,uqhd->ukhd", prob_low, grad_mixed)
    grad_scores = prob * (grad_prob - jnp.sum(grad_prob * prob, axis=-1, keepdims=True))
    grad_scores = grad_scores.astype(LOW)
    grad_query = rotate_back(ein("uhqk,ukhd->uqhd", grad_scores, keys) * scale, cosine, sine)
    grad_keys = rotate_back(ein("uhqk,uqhd->ukhd", grad_scores, query) * scale, cosine, sine)
    grad_projected = jnp.stack([grad_query, grad_keys, grad_values], axis=2).astype(LOW)
    grad_projected = grad_projected.reshape(team * count, 3 * att_share)
    qkv_grad = dot(normed_one, grad_projected, CONTRACT_FIRST)
    att_grad = grad_scatter(jnp.concatenate([qkv_grad, out_grad], axis=1).astype(LOW))
    grad_normed_one = dot(grad_projected, qkv_low, CONTRACT_LAST).astype(LOW)
    grad_normed_one = team_sum(grad_normed_one.reshape(team, count, width))
    grad_tokens = (grad_resid + normalize_back(flat, grad_normed_one)).reshape(units, length, width)
    fed = dot(hidden, down_low, CONTRACT_LAST).astype(LOW)
    fed = team_sum(fed.reshape(team, count, width))
    out_tokens = (resid + fed).astype(LOW).reshape(units, length, width)

    att_full_grad = jnp.concatenate(spread(att_grad, 4), axis=1)
    mlp_full_grad = jnp.concatenate(spread(gate_grad, 2) + spread(down_grad, 1), axis=1)

    def update(master, grad, first, second, outer):
        inner, one, two = adam_step(master, grad, first[0], second[0])
        diff = (master - inner).astype(LOW)
        total = diff.astype(FULL) + swap(diff).astype(FULL)
        mean = total / reps
        new, momentum = outer_step(master, mean, outer)
        return (new, one[None], two[None], mean, momentum)

    return (
        out_tokens,
        grad_tokens,
        *update(att_master, att_full_grad, att_first, att_second, att_outer),
        *update(mlp_master, mlp_full_grad, mlp_first, mlp_second, mlp_outer),
    )


def solution(mesh):
    in_specs = (
        P(("rep", "dp"), None, None),
        P(("rep", "dp"), None, None),
        P(("rep", "dp"), None),
        P("dp", None),
        P("rep", "dp", None),
        P("rep", "dp", None),
        P("dp", None),
        P("dp", None),
        P("rep", "dp", None),
        P("rep", "dp", None),
        P("dp", None),
    )
    out_specs = (
        P(("rep", "dp"), None, None),
        P(("rep", "dp"), None, None),
        P("dp", None),
        P("rep", "dp", None),
        P("rep", "dp", None),
        P("dp", None),
        P("dp", None),
        P("dp", None),
        P("rep", "dp", None),
        P("rep", "dp", None),
        P("dp", None),
        P("dp", None),
    )

    def body(*args):
        return on_device(mesh.shape["rep"], mesh.shape["dp"], *args)

    return jax.shard_map(
        body, mesh=mesh, in_specs=in_specs, out_specs=out_specs, check_vma=False
    )
```

time: 3520 us -> 1780 us (0.51)
  waiting for transfers between devices: 2860 us -> 547 us
  local copies, waits for them, and re-layouts: 70 us -> 473 us
  starting transfers between devices: 0.25 us -> 346 us
  matrix products: 294 us -> 163 us
  other arithmetic: 276 us -> 235 us
    unnamed x7 -> x0, waiting for transfers between devices: 1760 us -> none
    ppermute x0 -> x175, waiting for transfers between devices: none -> 547 us  [the longest x149 412 us: hop(): return lax.ppermute(values, ('rep', 'dp'), pairs)]
    all_gather x3 -> x0, waiting for transfers between devices: 542 us -> none  [the longest x1 250 us: on_device(): lax.all_gather(gate_part, 'dp', axis=0, tiled=True)]
    reduce_scatter x1 -> x0, waiting for transfers between devices: 393 us -> none  [on_device(): lax.psum_scatter(jnp.concatenate([first_block, second_block], axis=1), 'd...]
    ppermute x0 -> x175, starting transfers between devices: none -> 346 us  [the longest x149 319 us: hop(): return lax.ppermute(values, ('rep', 'dp'), pairs)]
    concatenate x2 -> x16, other arithmetic: 177 us -> 15.6 us  [the longest x5 8.15 us: share_out(): jnp.concatenate([low[:, base:base + team * share].reshape(rows, team, sha...]
    psum x1 -> x0, waiting for transfers between devices: 160 us -> none  [on_device(): lax.psum((att_master - att_inner).astype(jnp.bfloat16), 'rep')]
    dynamic_update_slice x0 -> x72, local copies, waits for them, and re-layouts: none -> 150 us  [the longest x24 67 us: weight_gather(): lax.dynamic_update_slice(result, part, (start + (1 - rep) * half, 0))]
  transfers between devices with their start and end apart: 6 -> 175, of which waited for: 6 -> 73; matrix products, arithmetic and copies ran while one was open for 12% -> 39% of each run, Pallas kernels for 0% -> 0%
where the time goes in v1:
time: 1780 us; the launch traced here: 1770 us
  waiting for transfers between devices  547 us (31%)
  local copies, waits for them, and re-layouts  473 us (27%)
  starting transfers between devices  346 us (19%)
  other arithmetic  235 us (13%)
  matrix products  163 us (9%)
    ppermute x149, waiting for transfers between devices, hop(): return lax.ppermute(values, ('rep', 'dp'), pairs)  412 us
    ppermute x149, starting transfers between devices, hop(): return lax.ppermute(values, ('rep', 'dp'), pairs)  319 us
    dot_general x12, matrix products, dot(): return lax.dot_general(left, right, dims, preferred_element_type=FULL)  154 us
    unnamed x302, local copies, waits for them, and re-layouts  152 us
    ppermute x26, waiting for transfers between devices, swap(): return lax.ppermute(values, ('rep', 'dp'), pairs)  135 us
    dynamic_update_slice x24, local copies, waits for them, and re-layouts, weight_gather(): lax.dynamic_update_slice(result, part, (start + (1 - rep) * half, 0))  67 us
    dynamic_update_slice x24, local copies, waits for them, and re-layouts, weight_gather(): result = lax.dynamic_update_slice(result, part, (start + rep * half, 0))  61.7 us
  transfers between devices with their start and end apart: 175, of which 73 were waited for; matrix products, arithmetic and copies ran while one was open for 39% of the time, Pallas kernels for 0%

profile of v1, /device:TPU:0, one launch (start us, length us, event | category | flops | bytes accessed | tf_op | source)
XLA Modules:
  0.0 1765.8 jit_solution(15743149730892446354)
XLA Ops:
  16.6 12.6 copy.329
  103.4 23.5 %collective-permute-done.19 = bf16[64,1024]{0,1:T(8,128)(2,1)S(1)} collective-permute-done((bf16[64,1024]{0,1:T(8,128)(2,1)}, bf16[64,1024]{0,1:T(8,128)(2,1)S(1)}, u32[]{:S(2)}, u32[]{:S(2)}) %collective-permute-start.19) | collective-permute-done | bytes 131104 | tf_op jit(solution)/shard_map/ppermute | solution.py:129
  129.8 11.7 collective-permute-done.21
  141.5 9.1 collective-permute-start.83
  150.6 12.0 collective-permute-start.85
  162.6 11.4 collective-permute-start.87
  211.3 12.6 copy.369
  223.9 12.6 copy.365
  236.5 12.8 copy.361
  258.7 7.2 collective-permute-done.89
  277.2 19.5 %collective-permute-start.11 = (bf16[128,1024]{0,1:T(8,128)(2,1)}, bf16[128,1024]{0,1:T(8,128)(2,1)S(1)}, u32[]{:S(2)}, u32[]{:S(2)}) collective-permute-start(bf16[128,1024]{0,1:T(8,128)(2,1)} %bitcast.571), channel_id=1, source_target_pairs={{0,4},{1,5},{2,6},{3,7},{4,0},{5,1},{6,2},{7,3},{8,12},{9,13},{10,... | collective-permute-start | bytes 786440 | tf_op jit(solution)/shard_map/ppermute | solution.py:129
  536.8 27.5 %collective-permute-done.55 = bf16[128,2048]{1,0:T(8,128)(2,1)S(1)} collective-permute-done((bf16[128,2048]{1,0:T(8,128)(2,1)}, bf16[128,2048]{1,0:T(8,128)(2,1)S(1)}, u32[]{:S(2)}, u32[]{:S(2)}) %collective-permute-start.55) | collective-permute-done | bytes 524320 | tf_op jit(solution)/shard_map/ppermute | solution.py:129
  566.6 10.5 collective-permute-done.56
  588.6 12.3 collective-permute-done.5
  617.2 9.1 fusion.10
  678.0 13.7 collective-permute-start.105
  708.0 7.4 collective-permute-done.105
  721.2 9.1 convert_add_fusion.3
  735.1 11.2 collective-permute-done.39
  754.2 18.9 %collective-permute-done.42 = bf16[256,2048]{1,0:T(8,128)(2,1)S(1)} collective-permute-done((bf16[256,2048]{1,0:T(8,128)(2,1)S(1)}, bf16[256,2048]{1,0:T(8,128)(2,1)S(1)}, u32[]{:S(2)}, u32[]{:S(2)}) %collective-permute-start.42) | collective-permute-done | bytes 1048608 | tf_op jit(solution)/shard_map/ppermute | solution.py:129
  782.0 21.3 %collective-permute-done.46 = bf16[256,2048]{1,0:T(8,128)(2,1)S(1)} collective-permute-done((bf16[256,2048]{1,0:T(8,128)(2,1)S(1)}, bf16[256,2048]{1,0:T(8,128)(2,1)S(1)}, u32[]{:S(2)}, u32[]{:S(2)}) %collective-permute-start.46) | collective-permute-done | bytes 1048608 | tf_op jit(solution)/shard_map/ppermute | solution.py:129
  806.3 10.3 collective-permute-done.48
  820.7 23.7 %fusion.140 = f32[2048,2048]{0,1:T(8,128)} fusion(bf16[2048,2048]{1,0:T(8,128)(2,1)S(1)} %bitcast.582, bf16[2048,2048]{1,0:T(8,128)(2,1)} %constant_dynamic-update-slice_fusion.16), kind=kOutput, calls=%fused_computation.511 | convolution fusion | flops 17179869184 | bytes 33554432 | tf_op jit(solution)/shard_map/dot_general | solution.py:97
  844.4 19.2 %multiply_convert_fusion.1 = (bf16[2048,1024]{0,1:T(8,128)(2,1)}, bf16[2048,1024]{0,1:T(8,128)(2,1)}, bf16[2048,1024]{0,1:T(8,128)(2,1)}) fusion(f32[2048,2048]{0,1:T(8,128)} %fusion.140, bf16[2048,2048]{1,0:T(8,128)(2,1)} %bitcast.580, bf16[2048,1024]{0,1:T(8,128)(2,1)S(1)} %copy-done.34), kind=kOutput, calls=%fused_computation.77 | convolution fusion | flops 8621391872 | bytes 41943040 | tf_op jit(solution)/shard_map/dot_general | solution.py:97
  863.6 11.4 convolution_convert_fusion.3
  875.0 14.3 convolution_convert_fusion.5
  889.3 23.8 %convolution_convert_fusion.2 = bf16[2048,2048]{1,0:T(8,128)(2,1)} fusion(bf16[2048,2048]{1,0:T(8,128)(2,1)} %constant_dynamic-update-slice_fusion.16, bf16[2048,1024]{0,1:T(8,128)(2,1)} %get-tuple-element.78, bf16[2048,1024]{0,1:T(8,128)(2,1)} %get-tuple-element.77), kind=kOutput, calls=%fused_computation.85 | convolution fusion | flops 17200840704 | bytes 25165824 | tf_op jit(solution)/shard_map/dot_general | solution.py:97
  913.2 23.8 %convolution_convert_fusion = bf16[2048,2048]{1,0:T(8,128)(2,1)} fusion(bf16[2048,2048]{1,0:T(8,128)(2,1)} %bitcast.583, bf16[2048,1024]{0,1:T(8,128)(2,1)} %get-tuple-element.78, bf16[2048,1024]{0,1:T(8,128)(2,1)} %get-tuple-element.77), kind=kOutput, calls=%fused_computation.83 | convolution fusion | flops 17200840704 | bytes 25165824 | tf_op jit(solution)/shard_map/dot_general | solution.py:97
  955.6 9.6 collective-permute-done.159
  967.0 9.1 collective-permute-done.161
  993.2 8.1 collective-permute-start.171
  1007.8 8.4 collective-permute-start.172
  1017.4 12.2 collective-permute-start.146
  1031.8 27.7 %collective-permute-start.148 = (bf16[128,2048]{1,0:T(8,128)(2,1)}, bf16[128,2048]{1,0:T(8,128)(2,1)}, u32[]{:S(2)}, u32[]{:S(2)}) collective-permute-start(bf16[128,2048]{1,0:T(8,128)(2,1)} %get-tuple-element.103), channel_id=1, source_target_pairs={{0,10},{1,11},{2,8},{3,9},{4,14},{5,15},{6,12},{7,13},{8,2},{9,3},... | collective-permute-start | bytes 1572872 | tf_op jit(solution)/shard_map/ppermute | solution.py:129
  1083.8 17.5 collective-permute-done.146
  1108.5 19.0 %collective-permute-done.148 = bf16[128,2048]{1,0:T(8,128)(2,1)} collective-permute-done((bf16[128,2048]{1,0:T(8,128)(2,1)}, bf16[128,2048]{1,0:T(8,128)(2,1)}, u32[]{:S(2)}, u32[]{:S(2)}) %collective-permute-start.148) | collective-permute-done | bytes 524320 | tf_op jit(solution)/shard_map/ppermute | solution.py:129
  1129.8 8.6 collective-permute-done.150
  1140.7 16.9 collective-permute-done.151
  1164.0 16.0 collective-permute-done.153
  1184.0 25.6 %collective-permute-start.157 = (bf16[128,2048]{1,0:T(8,128)(2,1)S(1)}, bf16[128,2048]{1,0:T(8,128)(2,1)S(1)}, u32[]{:S(2)}, u32[]{:S(2)}) collective-permute-start(bf16[128,2048]{1,0:T(8,128)(2,1)S(1)} %get-tuple-element.93), channel_id=1, source_target_pairs={{0,7},{1,6},{2,5},{3,4},{4,3},{5,2},{6,1},{7,0},{8,15},{9,14},{10,... | collective-permute-start | bytes 1572872 | tf_op jit(solution)/shard_map/ppermute | solution.py:129
  1211.8 17.2 collective-permute-done.157
  1230.2 8.0 gather_fusion
  1257.8 9.0 convert_add_fusion.1
  1272.2 9.4 convert_add_fusion.2
  1302.7 20.5 %fusion.7 = bf16[128,24576]{0,1:T(8,128)(2,1)} fusion(f32[128,24576]{0,1:T(8,128)S(1)} %bitcast.503, f32[128,8192]{0,1:T(8,128)} %bitcast.514, f32[128,8192]{0,1:T(8,128)} %bitcast.516, f32[128,8192]{0,1:T(8,128)} %bitcast.518, f32[1,128,24576]{1,2,0:T(8,128)} %copy.365, f32[1,128,24576]{1,2,0:T(8,128)} %copy.361), kind=kLoop, calls=%fused_computation.29 | loop fusion | flops 59768832 | bytes 56623104 | tf_op jit(solution)/shard_map/convert_element_type | solution.py:276
  1324.9 15.3 collective-permute-done.101
  1353.9 23.6 %fusion.8 = (f32[1,128,24576]{1,2,0:T(8,128)}, f32[1,128,24576]{1,2,0:T(8,128)}) fusion(f32[1,128,24576]{1,2,0:T(8,128)} %copy.365, f32[1,128,8192]{1,2,0:T(8,128)} %bitcast.515, f32[1,128,8192]{1,2,0:T(8,128)} %bitcast.517, f32[1,128,8192]{1,2,0:T(8,128)} %bitcast.519, f32[1,128,24576]{1,2,0:T(8,128)} %copy.361), kind=kLoop, calls=%fused_computation.30 | loop fusion | flops 28311552 | bytes 62914560 | tf_op jit(solution)/shard_map/add | solution.py:82
  1377.5 12.6 copy.375
  1390.1 12.6 copy.376
  1406.4 52.1 %collective-permute-done.174 = bf16[128,24576]{0,1:T(8,128)(2,1)} collective-permute-done((bf16[128,24576]{0,1:T(8,128)(2,1)}, bf16[128,24576]{0,1:T(8,128)(2,1)}, u32[]{:S(2)}, u32[]{:S(2)}) %collective-permute-start.174) | collective-permute-done | bytes 6291488 | tf_op jit(solution)/shard_map/ppermute | solution.py:133
  1458.5 26.3 %multiply_add_fusion.1 = (f32[128,24576]{0,1:T(8,128)}, f32[128,24576]{0,1:T(8,128)}, f32[128,24576]{0,1:T(8,128)}) fusion(f32[128,24576]{0,1:T(8,128)} %copy.369, bf16[128,24576]{0,1:T(8,128)(2,1)} %collective-permute-done.174, bf16[128,24576]{0,1:T(8,128)(2,1)} %fusion.7, f32[128,24576]{0,1:T(8,128)} %copy.329), kind=kLoop, calls=%fused_computation.37 | loop fusion | flops 31457280 | bytes 75497472 | tf_op jit(solution)/shard_map/add | solution.py:92
  1484.8 12.6 copy.374
  1497.4 12.6 copy.377
  1510.0 12.6 copy.378
  1556.4 9.6 convolution_convert_fusion.1
  1566.1 6.9 convolution_convert_fusion.6
  1581.6 18.8 %collective-permute-done.128 = bf16[128,1024]{0,1:T(8,128)(2,1)S(1)} collective-permute-done((bf16[128,1024]{0,1:T(8,128)(2,1)S(1)}, bf16[128,1024]{0,1:T(8,128)(2,1)S(1)}, u32[]{:S(2)}, u32[]{:S(2)}) %collective-permute-start.128) | collective-permute-done | bytes 262176 | tf_op jit(solution)/shard_map/ppermute | solution.py:129
  1607.6 9.7 collective-permute-done.132
  1622.0 7.4 collective-permute-start.138
  1643.3 7.0 collective-permute-done.137
  1685.0 8.7 fusion.19
  1701.0 8.1 convert_add_fusion
  1740.3 9.5 multiply_subtract_fusion.1
  1749.8 7.1 collective-permute-done.127
  (880 shorter events, 834.4 us)
Async XLA Ops:
  0.6 81.6 %collective-permute-start.31 = (s32[1,2]{1,0:T(1,128)}, s32[1,2]{1,0:T(1,128)}, u32[]{:S(2)}, u32[]{:S(2)}) collective-permute-start(s32[1,2]{1,0:T(1,128)} %param.15), channel_id=1, source_target_pairs={{0,1},{1,0},{2,3},{3,2},{4,5},{5,4},{6,7},{7,6},{8,9},{9,8},{10,11... | collective-permute-start | bytes 32 | tf_op jit(solution)/shard_map/ppermute | solution.py:129
  1.2 82.7 %collective-permute-start.32 = (s32[1,2]{1,0:T(1,128)}, s32[1,2]{1,0:T(1,128)}, u32[]{:S(2)}, u32[]{:S(2)}) collective-permute-start(s32[1,2]{1,0:T(1,128)} %param.15), channel_id=1, source_target_pairs={{0,2},{1,3},{2,0},{3,1},{4,6},{5,7},{6,4},{7,5},{8,10},{9,11},{10,... | collective-permute-start | bytes 32 | tf_op jit(solution)/shard_map/ppermute | solution.py:129
  3.8 80.2 %collective-permute-start.33 = (s32[1,2]{1,0:T(1,128)}, s32[1,2]{1,0:T(1,128)}, u32[]{:S(2)}, u32[]{:S(2)}) collective-permute-start(s32[1,2]{1,0:T(1,128)} %param.15), channel_id=1, source_target_pairs={{0,3},{1,2},{2,1},{3,0},{4,7},{5,6},{6,5},{7,4},{8,11},{9,10},{10,... | collective-permute-start | bytes 32 | tf_op jit(solution)/shard_map/ppermute | solution.py:129
  12.9 81.8 %collective-permute-start.15 = (bf16[64,1024]{0,1:T(8,128)(2,1)}, bf16[64,1024]{0,1:T(8,128)(2,1)}, u32[]{:S(2)}, u32[]{:S(2)}) collective-permute-start(bf16[64,1024]{0,1:T(8,128)(2,1)} %bitcast.22), channel_id=1, source_target_pairs={{0,8},{1,9},{2,10},{3,11},{4,12},{5,13},{6,14},{7,15},{8,0},{9,1},... | collective-permute-start | bytes 393224 | tf_op jit(solution)/shard_map/ppermute | solution.py:129
  16.6 78.9 %collective-permute-start.17 = (bf16[64,1024]{0,1:T(8,128)(2,1)}, bf16[64,1024]{0,1:T(8,128)(2,1)}, u32[]{:S(2)}, u32[]{:S(2)}) collective-permute-start(bf16[64,1024]{0,1:T(8,128)(2,1)} %bitcast.23), channel_id=1, source_target_pairs={{0,9},{1,8},{2,11},{3,10},{4,13},{5,12},{6,15},{7,14},{8,1},{9,0},... | collective-permute-start | bytes 393224 | tf_op jit(solution)/shard_map/ppermute | solution.py:129
  87.8 39.0 %collective-permute-start.19 = (bf16[64,1024]{0,1:T(8,128)(2,1)}, bf16[64,1024]{0,1:T(8,128)(2,1)S(1)}, u32[]{:S(2)}, u32[]{:S(2)}) collective-permute-start(bf16[64,1024]{0,1:T(8,128)(2,1)} %bitcast.576), channel_id=1, source_target_pairs={{0,10},{1,11},{2,8},{3,9},{4,14},{5,15},{6,12},{7,13},{8,2},{9,3},... | collective-permute-start | bytes 393224 | tf_op jit(solution)/shard_map/ppermute | solution.py:129
  91.0 50.5 %collective-permute-start.21 = (bf16[64,1024]{0,1:T(8,128)(2,1)}, bf16[64,1024]{0,1:T(8,128)(2,1)}, u32[]{:S(2)}, u32[]{:S(2)}) collective-permute-start(bf16[64,1024]{0,1:T(8,128)(2,1)} %bitcast.575), channel_id=1, source_target_pairs={{0,11},{1,10},{2,9},{3,8},{4,15},{5,14},{6,13},{7,12},{8,3},{9,2},... | collective-permute-start | bytes 393224 | tf_op jit(solution)/shard_map/ppermute | solution.py:129
  92.2 49.3 %collective-permute-start.23 = (bf16[64,1024]{0,1:T(8,128)(2,1)}, bf16[64,1024]{0,1:T(8,128)(2,1)}, u32[]{:S(2)}, u32[]{:S(2)}) collective-permute-start(bf16[64,1024]{0,1:T(8,128)(2,1)} %bitcast.574), channel_id=1, source_target_pairs={{0,12},{1,13},{2,14},{3,15},{4,8},{5,9},{6,10},{7,11},{8,4},{9,5},... | collective-permute-start | bytes 393224 | tf_op jit(solution)/shard_map/ppermute | solution.py:129
  94.7 55.9 %collective-permute-start.25 = (bf16[64,1024]{0,1:T(8,128)(2,1)}, bf16[64,1024]{0,1:T(8,128)(2,1)}, u32[]{:S(2)}, u32[]{:S(2)}) collective-permute-start(bf16[64,1024]{0,1:T(8,128)(2,1)} %bitcast.573), channel_id=1, source_target_pairs={{0,13},{1,12},{2,15},{3,14},{4,9},{5,8},{6,11},{7,10},{8,5},{9,4},... | collective-permute-start | bytes 393224 | tf_op jit(solution)/shard_map/ppermute | solution.py:129
  95.4 67.1 %collective-permute-start.27 = (bf16[64,1024]{0,1:T(8,128)(2,1)}, bf16[64,1024]{0,1:T(8,128)(2,1)}, u32[]{:S(2)}, u32[]{:S(2)}) collective-permute-start(bf16[64,1024]{0,1:T(8,128)(2,1)} %bitcast.572), channel_id=1, source_target_pairs={{0,14},{1,15},{2,12},{3,13},{4,10},{5,11},{6,8},{7,9},{8,6},{9,7},... | collective-permute-start | bytes 393224 | tf_op jit(solution)/shard_map/ppermute | solution.py:129
  126.9 125.3 %collective-permute-start.29 = (bf16[64,1024]{0,1:T(8,128)(2,1)}, bf16[64,1024]{0,1:T(8,128)(2,1)}, u32[]{:S(2)}, u32[]{:S(2)}) collective-permute-start(bf16[64,1024]{0,1:T(8,128)(2,1)} %bitcast.29), channel_id=1, source_target_pairs={{0,15},{1,14},{2,13},{3,12},{4,11},{5,10},{6,9},{7,8},{8,7},{9,6},... | collective-permute-start | bytes 393224 | tf_op jit(solution)/shard_map/ppermute | solution.py:129
  141.5 111.9 %collective-permute-start.81 = (bf16[64,1024]{0,1:T(8,128)(2,1)}, bf16[64,1024]{0,1:T(8,128)(2,1)}, u32[]{:S(2)}, u32[]{:S(2)}) collective-permute-start(bf16[64,1024]{0,1:T(8,128)(2,1)} %get-tuple-element.205), channel_id=1, source_target_pairs={{0,8},{1,9},{2,10},{3,11},{4,12},{5,13},{6,14},{7,15},{8,0},{9,1},... | collective-permute-start | bytes 393224 | tf_op jit(solution)/shard_map/ppermute | solution.py:129
  141.5 112.5 %collective-permute-start.83 = (bf16[64,1024]{0,1:T(8,128)(2,1)}, bf16[64,1024]{0,1:T(8,128)(2,1)}, u32[]{:S(2)}, u32[]{:S(2)}) collective-permute-start(bf16[64,1024]{0,1:T(8,128)(2,1)} %get-tuple-element.204), channel_id=1, source_target_pairs={{0,9},{1,8},{2,11},{3,10},{4,13},{5,12},{6,15},{7,14},{8,1},{9,0},... | collective-permute-start | bytes 393224 | tf_op jit(solution)/shard_map/ppermute | solution.py:129
  150.6 104.3 %collective-permute-start.85 = (bf16[64,1024]{0,1:T(8,128)(2,1)}, bf16[64,1024]{0,1:T(8,128)(2,1)}, u32[]{:S(2)}, u32[]{:S(2)}) collective-permute-start(bf16[64,1024]{0,1:T(8,128)(2,1)} %get-tuple-element.203), channel_id=1, source_target_pairs={{0,10},{1,11},{2,8},{3,9},{4,14},{5,15},{6,12},{7,13},{8,2},{9,3},... | collective-permute-start | bytes 393224 | tf_op jit(solution)/shard_map/ppermute | solution.py:129
  162.6 92.9 %collective-permute-start.87 = (bf16[64,1024]{0,1:T(8,128)(2,1)}, bf16[64,1024]{0,1:T(8,128)(2,1)}, u32[]{:S(2)}, u32[]{:S(2)}) collective-permute-start(bf16[64,1024]{0,1:T(8,128)(2,1)} %get-tuple-element.202), channel_id=1, source_target_pairs={{0,11},{1,10},{2,9},{3,8},{4,15},{5,14},{6,13},{7,12},{8,3},{9,2},... | collective-permute-start | bytes 393224 | tf_op jit(solution)/shard_map/ppermute | solution.py:129
  252.2 49.2 %collective-permute-start.8 = (bf16[128,1024]{0,1:T(8,128)(2,1)}, bf16[128,1024]{0,1:T(8,128)(2,1)S(1)}, u32[]{:S(2)}, u32[]{:S(2)}) collective-permute-start(bf16[128,1024]{0,1:T(8,128)(2,1)} %bitcast.15), channel_id=1, source_target_pairs={{0,1},{1,0},{2,3},{3,2},{4,5},{5,4},{6,7},{7,6},{8,9},{9,8},{10,11... | collective-permute-start | bytes 786440 | tf_op jit(solution)/shard_map/ppermute | solution.py:129
  253.4 48.3 %collective-permute-start.9 = (bf16[128,1024]{0,1:T(8,128)(2,1)}, bf16[128,1024]{0,1:T(8,128)(2,1)S(1)}, u32[]{:S(2)}, u32[]{:S(2)}) collective-permute-start(bf16[128,1024]{0,1:T(8,128)(2,1)} %bitcast.16), channel_id=1, source_target_pairs={{0,2},{1,3},{2,0},{3,1},{4,6},{5,7},{6,4},{7,5},{8,10},{9,11},{10,... | collective-permute-start | bytes 786440 | tf_op jit(solution)/shard_map/ppermute | solution.py:129
  254.1 47.8 %collective-permute-start.10 = (bf16[128,1024]{0,1:T(8,128)(2,1)}, bf16[128,1024]{0,1:T(8,128)(2,1)S(1)}, u32[]{:S(2)}, u32[]{:S(2)}) collective-permute-start(bf16[128,1024]{0,1:T(8,128)(2,1)} %bitcast.17), channel_id=1, source_target_pairs={{0,3},{1,2},{2,1},{3,0},{4,7},{5,6},{6,5},{7,4},{8,11},{9,10},{10,... | collective-permute-start | bytes 786440 | tf_op jit(solution)/shard_map/ppermute | solution.py:129
  364.2 161.1 %collective-permute-start.51 = (bf16[128,2048]{1,0:T(8,128)(2,1)}, bf16[128,2048]{1,0:T(8,128)(2,1)}, u32[]{:S(2)}, u32[]{:S(2)}) collective-permute-start(bf16[128,2048]{1,0:T(8,128)(2,1)} %bitcast.68), channel_id=1, source_target_pairs={{0,1},{1,0},{2,3},{3,2},{4,5},{5,4},{6,7},{7,6},{8,9},{9,8},{10,11... | collective-permute-start | bytes 1572872 | tf_op jit(solution)/shard_map/ppermute | solution.py:129
  378.8 149.8 %collective-permute-start.52 = (bf16[128,2048]{1,0:T(8,128)(2,1)}, bf16[128,2048]{1,0:T(8,128)(2,1)}, u32[]{:S(2)}, u32[]{:S(2)}) collective-permute-start(bf16[128,2048]{1,0:T(8,128)(2,1)} %bitcast.69), channel_id=1, source_target_pairs={{0,2},{1,3},{2,0},{3,1},{4,6},{5,7},{6,4},{7,5},{8,10},{9,11},{10,... | collective-permute-start | bytes 1572872 | tf_op jit(solution)/shard_map/ppermute | solution.py:129
  384.4 144.7 %collective-permute-start.53 = (bf16[128,2048]{1,0:T(8,128)(2,1)}, bf16[128,2048]{1,0:T(8,128)(2,1)}, u32[]{:S(2)}, u32[]{:S(2)}) collective-permute-start(bf16[128,2048]{1,0:T(8,128)(2,1)} %bitcast.70), channel_id=1, source_target_pairs={{0,3},{1,2},{2,1},{3,0},{4,7},{5,6},{6,5},{7,4},{8,11},{9,10},{10,... | collective-permute-start | bytes 1572872 | tf_op jit(solution)/shard_map/ppermute | solution.py:129
  395.6 126.1 %collective-permute-start.96 = (bf16[64,1024]{0,1:T(8,128)(2,1)}, bf16[64,1024]{0,1:T(8,128)(2,1)}, u32[]{:S(2)}, u32[]{:S(2)}) collective-permute-start(bf16[64,1024]{0,1:T(8,128)(2,1)} %collective-permute-done.95), channel_id=1, source_target_pairs={{0,16},{1,17},{2,18},{3,19},{4,20},{5,21},{6,22},{7,23},{8,24},{9,... | collective-permute-start | bytes 393224 | tf_op jit(solution)/shard_map/ppermute | solution.py:133
  401.3 130.7 %collective-permute-start.54 = (bf16[128,2048]{1,0:T(8,128)(2,1)}, bf16[128,2048]{1,0:T(8,128)(2,1)}, u32[]{:S(2)}, u32[]{:S(2)}) collective-permute-start(bf16[128,2048]{1,0:T(8,128)(2,1)} %bitcast.71), channel_id=1, source_target_pairs={{0,4},{1,5},{2,6},{3,7},{4,0},{5,1},{6,2},{7,3},{8,12},{9,13},{10,... | collective-permute-start | bytes 1572872 | tf_op jit(solution)/shard_map/ppermute | solution.py:129
  521.8 63.4 %collective-permute-start = (bf16[256,2048]{1,0:T(8,128)(2,1)S(1)}, bf16[256,2048]{1,0:T(8,128)(2,1)}, u32[]{:S(2)}, u32[]{:S(2)}) collective-permute-start(bf16[256,2048]{1,0:T(8,128)(2,1)S(1)} %copy-done.49), channel_id=1, source_target_pairs={{0,1},{1,0},{2,3},{3,2},{4,5},{5,4},{6,7},{7,6},{8,9},{9,8},{10,11... | collective-permute-start | bytes 3145736 | tf_op jit(solution)/shard_map/ppermute | solution.py:129
  525.2 58.4 %collective-permute-start.1 = (bf16[256,2048]{1,0:T(8,128)(2,1)S(1)}, bf16[256,2048]{1,0:T(8,128)(2,1)S(1)}, u32[]{:S(2)}, u32[]{:S(2)}) collective-permute-start(bf16[256,2048]{1,0:T(8,128)(2,1)S(1)} %copy-done.49), channel_id=1, source_target_pairs={{0,2},{1,3},{2,0},{3,1},{4,6},{5,7},{6,4},{7,5},{8,10},{9,11},{10,... | collective-permute-start | bytes 3145736 | tf_op jit(solution)/shard_map/ppermute | solution.py:129
  528.5 53.6 %collective-permute-start.3 = (bf16[256,2048]{1,0:T(8,128)(2,1)S(1)}, bf16[256,2048]{1,0:T(8,128)(2,1)S(1)}, u32[]{:S(2)}, u32[]{:S(2)}) collective-permute-start(bf16[256,2048]{1,0:T(8,128)(2,1)S(1)} %copy-done.49), channel_id=1, source_target_pairs={{0,4},{1,5},{2,6},{3,7},{4,0},{5,1},{6,2},{7,3},{8,12},{9,13},{10,... | collective-permute-start | bytes 3145736 | tf_op jit(solution)/shard_map/ppermute | solution.py:129
  532.0 45.2 %collective-permute-start.56 = (bf16[128,2048]{1,0:T(8,128)(2,1)}, bf16[128,2048]{1,0:T(8,128)(2,1)S(1)}, u32[]{:S(2)}, u32[]{:S(2)}) collective-permute-start(bf16[128,2048]{1,0:T(8,128)(2,1)} %bitcast.558), channel_id=1, source_target_pairs={{0,6},{1,7},{2,4},{3,5},{4,2},{5,3},{6,0},{7,1},{8,14},{9,15},{10,... | collective-permute-start | bytes 1572872 | tf_op jit(solution)/shard_map/ppermute | solution.py:129
  564.3 75.5 %collective-permute-start.57 = (bf16[128,2048]{1,0:T(8,128)(2,1)S(1)}, bf16[128,2048]{1,0:T(8,128)(2,1)S(1)}, u32[]{:S(2)}, u32[]{:S(2)}) collective-permute-start(bf16[128,2048]{1,0:T(8,128)(2,1)S(1)} %bitcast.557), channel_id=1, source_target_pairs={{0,7},{1,6},{2,5},{3,4},{4,3},{5,2},{6,1},{7,0},{8,15},{9,14},{10,... | collective-permute-start | bytes 1572872 | tf_op jit(solution)/shard_map/ppermute | solution.py:129
  577.1 37.4 %collective-permute-start.58 = (bf16[64,2048]{1,0:T(8,128)(2,1)S(1)}, bf16[64,2048]{1,0:T(8,128)(2,1)S(1)}, u32[]{:S(2)}, u32[]{:S(2)}) collective-permute-start(bf16[64,2048]{1,0:T(8,128)(2,1)S(1)} %bitcast.567), channel_id=1, source_target_pairs={{0,8},{1,9},{2,10},{3,11},{4,12},{5,13},{6,14},{7,15},{8,0},{9,1},... | collective-permute-start | bytes 786440 | tf_op jit(solution)/shard_map/ppermute | solution.py:129
  601.0 40.5 %collective-permute-start.60 = (bf16[64,2048]{1,0:T(8,128)(2,1)S(1)}, bf16[64,2048]{1,0:T(8,128)(2,1)S(1)}, u32[]{:S(2)}, u32[]{:S(2)}) collective-permute-start(bf16[64,2048]{1,0:T(8,128)(2,1)S(1)} %bitcast.566), channel_id=1, source_target_pairs={{0,9},{1,8},{2,11},{3,10},{4,13},{5,12},{6,15},{7,14},{8,1},{9,0},... | collective-permute-start | bytes 786440 | tf_op jit(solution)/shard_map/ppermute | solution.py:129
  607.2 40.9 %collective-permute-start.62 = (bf16[64,2048]{1,0:T(8,128)(2,1)S(1)}, bf16[64,2048]{1,0:T(8,128)(2,1)S(1)}, u32[]{:S(2)}, u32[]{:S(2)}) collective-permute-start(bf16[64,2048]{1,0:T(8,128)(2,1)S(1)} %bitcast.565), channel_id=1, source_target_pairs={{0,10},{1,11},{2,8},{3,9},{4,14},{5,15},{6,12},{7,13},{8,2},{9,3},... | collective-permute-start | bytes 786440 | tf_op jit(solution)/shard_map/ppermute | solution.py:129
  614.6 41.5 %collective-permute-start.64 = (bf16[64,2048]{1,0:T(8,128)(2,1)S(1)}, bf16[64,2048]{1,0:T(8,128)(2,1)S(1)}, u32[]{:S(2)}, u32[]{:S(2)}) collective-permute-start(bf16[64,2048]{1,0:T(8,128)(2,1)S(1)} %bitcast.564), channel_id=1, source_target_pairs={{0,11},{1,10},{2,9},{3,8},{4,15},{5,14},{6,13},{7,12},{8,3},{9,2},... | collective-permute-start | bytes 786440 | tf_op jit(solution)/shard_map/ppermute | solution.py:129
  639.9 81.3 %collective-permute-start.38 = (bf16[4,256,2048]{2,1,0:T(8,128)(2,1)S(1)}, bf16[4,256,2048]{2,1,0:T(8,128)(2,1)}, u32[]{:S(2)}, u32[]{:S(2)}) collective-permute-start(bf16[4,256,2048]{2,1,0:T(8,128)(2,1)S(1)} %slice.249), channel_id=1, source_target_pairs={{0,1},{1,0},{2,3},{3,2},{4,5},{5,4},{6,7},{7,6},{8,9},{9,8},{10,11... | collective-permute-start | bytes 12582920 | tf_op jit(solution)/shard_map/ppermute | solution.py:129
  669.5 50.6 %collective-permute-start.102 = (bf16[256,2048]{1,0:T(8,128)(2,1)S(1)}, bf16[256,2048]{1,0:T(8,128)(2,1)S(1)}, u32[]{:S(2)}, u32[]{:S(2)}) collective-permute-start(bf16[256,2048]{1,0:T(8,128)(2,1)S(1)} %bitcast.543), channel_id=1, source_target_pairs={{0,1},{1,0},{2,3},{3,2},{4,5},{5,4},{6,7},{7,6},{8,9},{9,8},{10,11... | collective-permute-start | bytes 3145736 | tf_op jit(solution)/shard_map/ppermute | solution.py:129
  676.4 41.1 %collective-permute-start.103 = (bf16[256,2048]{1,0:T(8,128)(2,1)S(1)}, bf16[256,2048]{1,0:T(8,128)(2,1)S(1)}, u32[]{:S(2)}, u32[]{:S(2)}) collective-permute-start(bf16[256,2048]{1,0:T(8,128)(2,1)S(1)} %bitcast.544), channel_id=1, source_target_pairs={{0,2},{1,3},{2,0},{3,1},{4,6},{5,7},{6,4},{7,5},{8,10},{9,11},{10,... | collective-permute-start | bytes 3145736 | tf_op jit(solution)/shard_map/ppermute | solution.py:129
  678.0 37.3 %collective-permute-start.105 = (bf16[256,2048]{1,0:T(8,128)(2,1)S(1)}, bf16[256,2048]{1,0:T(8,128)(2,1)S(1)}, u32[]{:S(2)}, u32[]{:S(2)}) collective-permute-start(bf16[256,2048]{1,0:T(8,128)(2,1)S(1)} %bitcast.545), channel_id=1, source_target_pairs={{0,4},{1,5},{2,6},{3,7},{4,0},{5,1},{6,2},{7,3},{8,12},{9,13},{10,... | collective-permute-start | bytes 3145736 | tf_op jit(solution)/shard_map/ppermute | solution.py:129
  734.0 44.7 %collective-permute-start.106 = (bf16[256,2048]{1,0:T(8,128)(2,1)S(1)}, bf16[256,2048]{1,0:T(8,128)(2,1)S(1)}, u32[]{:S(2)}, u32[]{:S(2)}) collective-permute-start(bf16[256,2048]{1,0:T(8,128)(2,1)S(1)} %collective-permute-done.105), channel_id=1, source_target_pairs={{0,1},{1,0},{2,3},{3,2},{4,5},{5,4},{6,7},{7,6},{8,9},{9,8},{10,11... | collective-permute-start | bytes 3145736 | tf_op jit(solution)/shard_map/ppermute | solution.py:129
  941.7 40.6 %collective-permute-start.163 = (bf16[128,1024]{1,0:T(8,128)(2,1)}, bf16[128,1024]{1,0:T(8,128)(2,1)}, u32[]{:S(2)}, u32[]{:S(2)}) collective-permute-start(bf16[128,1024]{1,0:T(8,128)(2,1)} %get-tuple-element.131), channel_id=1, source_target_pairs={{0,10},{1,11},{2,8},{3,9},{4,14},{5,15},{6,12},{7,13},{8,2},{9,3},... | collective-permute-start | bytes 786440 | tf_op jit(solution)/shard_map/ppermute | solution.py:129
  942.9 43.3 %collective-permute-start.162 = (bf16[128,1024]{1,0:T(8,128)(2,1)}, bf16[128,1024]{1,0:T(8,128)(2,1)}, u32[]{:S(2)}, u32[]{:S(2)}) collective-permute-start(bf16[128,1024]{1,0:T(8,128)(2,1)} %get-tuple-element.132), channel_id=1, source_target_pairs={{0,2},{1,3},{2,0},{3,1},{4,6},{5,7},{6,4},{7,5},{8,10},{9,11},{10,... | collective-permute-start | bytes 786440 | tf_op jit(solution)/shard_map/ppermute | solution.py:129
  1007.8 51.7 %collective-permute-start.172 = (bf16[128,1024]{1,0:T(8,128)(2,1)S(1)}, bf16[128,1024]{1,0:T(8,128)(2,1)S(1)}, u32[]{:S(2)}, u32[]{:S(2)}) collective-permute-start(bf16[128,1024]{1,0:T(8,128)(2,1)S(1)} %get-tuple-element.121), channel_id=1, source_target_pairs={{0,7},{1,6},{2,5},{3,4},{4,3},{5,2},{6,1},{7,0},{8,15},{9,14},{10,... | collective-permute-start | bytes 786440 | tf_op jit(solution)/shard_map/ppermute | solution.py:129
  1016.6 62.6 %collective-permute-start.144 = (bf16[128,2048]{1,0:T(8,128)(2,1)}, bf16[128,2048]{1,0:T(8,128)(2,1)}, u32[]{:S(2)}, u32[]{:S(2)}) collective-permute-start(bf16[128,2048]{1,0:T(8,128)(2,1)} %get-tuple-element.107), channel_id=1, source_target_pairs={{0,8},{1,9},{2,10},{3,11},{4,12},{5,13},{6,14},{7,15},{8,0},{9,1},... | collective-permute-start | bytes 1572872 | tf_op jit(solution)/shard_map/ppermute | solution.py:129
  1017.4 83.9 %collective-permute-start.146 = (bf16[128,2048]{1,0:T(8,128)(2,1)}, bf16[128,2048]{1,0:T(8,128)(2,1)}, u32[]{:S(2)}, u32[]{:S(2)}) collective-permute-start(bf16[128,2048]{1,0:T(8,128)(2,1)} %get-tuple-element.105), channel_id=1, source_target_pairs={{0,9},{1,8},{2,11},{3,10},{4,13},{5,12},{6,15},{7,14},{8,1},{9,0},... | collective-permute-start | bytes 1572872 | tf_op jit(solution)/shard_map/ppermute | solution.py:129
  1029.6 75.6 %collective-permute-start.145 = (bf16[128,2048]{1,0:T(8,128)(2,1)}, bf16[128,2048]{1,0:T(8,128)(2,1)}, u32[]{:S(2)}, u32[]{:S(2)}) collective-permute-start(bf16[128,2048]{1,0:T(8,128)(2,1)} %get-tuple-element.106), channel_id=1, source_target_pairs={{0,1},{1,0},{2,3},{3,2},{4,5},{5,4},{6,7},{7,6},{8,9},{9,8},{10,11... | collective-permute-start | bytes 1572872 | tf_op jit(solution)/shard_map/ppermute | solution.py:129
  1031.8 95.6 %collective-permute-start.148 = (bf16[128,2048]{1,0:T(8,128)(2,1)}, bf16[128,2048]{1,0:T(8,128)(2,1)}, u32[]{:S(2)}, u32[]{:S(2)}) collective-permute-start(bf16[128,2048]{1,0:T(8,128)(2,1)} %get-tuple-element.103), channel_id=1, source_target_pairs={{0,10},{1,11},{2,8},{3,9},{4,14},{5,15},{6,12},{7,13},{8,2},{9,3},... | collective-permute-start | bytes 1572872 | tf_op jit(solution)/shard_map/ppermute | solution.py:129
  1059.5 68.0 %collective-permute-start.147 = (bf16[128,2048]{1,0:T(8,128)(2,1)}, bf16[128,2048]{1,0:T(8,128)(2,1)}, u32[]{:S(2)}, u32[]{:S(2)}) collective-permute-start(bf16[128,2048]{1,0:T(8,128)(2,1)} %get-tuple-element.104), channel_id=1, source_target_pairs={{0,2},{1,3},{2,0},{3,1},{4,6},{5,7},{6,4},{7,5},{8,10},{9,11},{10,... | collective-permute-start | bytes 1572872 | tf_op jit(solution)/shard_map/ppermute | solution.py:129
  1079.1 59.3 %collective-permute-start.150 = (bf16[128,2048]{1,0:T(8,128)(2,1)}, bf16[128,2048]{1,0:T(8,128)(2,1)S(1)}, u32[]{:S(2)}, u32[]{:S(2)}) collective-permute-start(bf16[128,2048]{1,0:T(8,128)(2,1)} %get-tuple-element.101), channel_id=1, source_target_pairs={{0,11},{1,10},{2,9},{3,8},{4,15},{5,14},{6,13},{7,12},{8,3},{9,2},... | collective-permute-start | bytes 1572872 | tf_op jit(solution)/shard_map/ppermute | solution.py:129
  1101.3 37.7 %collective-permute-start.149 = (bf16[128,2048]{1,0:T(8,128)(2,1)S(1)}, bf16[128,2048]{1,0:T(8,128)(2,1)S(1)}, u32[]{:S(2)}, u32[]{:S(2)}) collective-permute-start(bf16[128,2048]{1,0:T(8,128)(2,1)S(1)} %copy-done.55), channel_id=1, source_target_pairs={{0,3},{1,2},{2,1},{3,0},{4,7},{5,6},{6,5},{7,4},{8,11},{9,10},{10,... | collective-permute-start | bytes 1572872 | tf_op jit(solution)/shard_map/ppermute | solution.py:129
  1127.4 130.4 %collective-permute-start.110 = (bf16[4,256,2048]{2,1,0:T(8,128)(2,1)}, bf16[4,256,2048]{2,1,0:T(8,128)(2,1)}, u32[]{:S(2)}, u32[]{:S(2)}) collective-permute-start(bf16[4,256,2048]{2,1,0:T(8,128)(2,1)} %slice.276), channel_id=1, source_target_pairs={{0,1},{1,0},{2,3},{3,2},{4,5},{5,4},{6,7},{7,6},{8,9},{9,8},{10,11... | collective-permute-start | bytes 12582920 | tf_op jit(solution)/shard_map/ppermute | solution.py:129
  1139.0 41.0 %collective-permute-start.153 = (bf16[128,2048]{1,0:T(8,128)(2,1)S(1)}, bf16[128,2048]{1,0:T(8,128)(2,1)S(1)}, u32[]{:S(2)}, u32[]{:S(2)}) collective-permute-start(bf16[128,2048]{1,0:T(8,128)(2,1)S(1)} %copy-done.51), channel_id=1, source_target_pairs={{0,5},{1,4},{2,7},{3,6},{4,1},{5,0},{6,3},{7,2},{8,13},{9,12},{10,... | collective-permute-start | bytes 1572872 | tf_op jit(solution)/shard_map/ppermute | solution.py:129
  1139.0 45.0 %collective-permute-start.156 = (bf16[128,2048]{1,0:T(8,128)(2,1)S(1)}, bf16[128,2048]{1,0:T(8,128)(2,1)S(1)}, u32[]{:S(2)}, u32[]{:S(2)}) collective-permute-start(bf16[128,2048]{1,0:T(8,128)(2,1)S(1)} %copy-done.50), channel_id=1, source_target_pairs={{0,14},{1,15},{2,12},{3,13},{4,10},{5,11},{6,8},{7,9},{8,6},{9,7},... | collective-permute-start | bytes 1572872 | tf_op jit(solution)/shard_map/ppermute | solution.py:129
  1157.6 53.1 %collective-permute-start.155 = (bf16[128,2048]{1,0:T(8,128)(2,1)S(1)}, bf16[128,2048]{1,0:T(8,128)(2,1)S(1)}, u32[]{:S(2)}, u32[]{:S(2)}) collective-permute-start(bf16[128,2048]{1,0:T(8,128)(2,1)S(1)} %get-tuple-element.96), channel_id=1, source_target_pairs={{0,6},{1,7},{2,4},{3,5},{4,2},{5,3},{6,0},{7,1},{8,14},{9,15},{10,... | collective-permute-start | bytes 1572872 | tf_op jit(solution)/shard_map/ppermute | solution.py:129
  1164.0 108.2 %collective-permute-start.97 = (bf16[4,256,2048]{2,1,0:T(8,128)(2,1)}, bf16[4,256,2048]{2,1,0:T(8,128)(2,1)}, u32[]{:S(2)}, u32[]{:S(2)}) collective-permute-start(bf16[4,256,2048]{2,1,0:T(8,128)(2,1)} %slice.265), channel_id=1, source_target_pairs={{0,1},{1,0},{2,3},{3,2},{4,5},{5,4},{6,7},{7,6},{8,9},{9,8},{10,11... | collective-permute-start | bytes 12582920 | tf_op jit(solution)/shard_map/ppermute | solution.py:129
  1184.0 45.0 %collective-permute-start.157 = (bf16[128,2048]{1,0:T(8,128)(2,1)S(1)}, bf16[128,2048]{1,0:T(8,128)(2,1)S(1)}, u32[]{:S(2)}, u32[]{:S(2)}) collective-permute-start(bf16[128,2048]{1,0:T(8,128)(2,1)S(1)} %get-tuple-element.93), channel_id=1, source_target_pairs={{0,7},{1,6},{2,5},{3,4},{4,3},{5,2},{6,1},{7,0},{8,15},{9,14},{10,... | collective-permute-start | bytes 1572872 | tf_op jit(solution)/shard_map/ppermute | solution.py:129
  1299.7 40.5 %collective-permute-start.101 = (bf16[256,2048]{1,0:T(8,128)(2,1)}, bf16[256,2048]{1,0:T(8,128)(2,1)}, u32[]{:S(2)}, u32[]{:S(2)}) collective-permute-start(bf16[256,2048]{1,0:T(8,128)(2,1)} %pad_maximum_fusion.13), channel_id=1, source_target_pairs={{0,4},{1,5},{2,6},{3,7},{4,0},{5,1},{6,2},{7,3},{8,12},{9,13},{10,... | collective-permute-start | bytes 3145736 | tf_op jit(solution)/shard_map/ppermute | solution.py:129
  1302.6 37.9 %collective-permute-start.99 = (bf16[256,2048]{1,0:T(8,128)(2,1)}, bf16[256,2048]{1,0:T(8,128)(2,1)}, u32[]{:S(2)}, u32[]{:S(2)}) collective-permute-start(bf16[256,2048]{1,0:T(8,128)(2,1)} %pad_maximum_fusion.12), channel_id=1, source_target_pairs={{0,2},{1,3},{2,0},{3,1},{4,6},{5,7},{6,4},{7,5},{8,10},{9,11},{10,... | collective-permute-start | bytes 3145736 | tf_op jit(solution)/shard_map/ppermute | solution.py:129
  1323.2 135.3 %collective-permute-start.174 = (bf16[128,24576]{0,1:T(8,128)(2,1)}, bf16[128,24576]{0,1:T(8,128)(2,1)}, u32[]{:S(2)}, u32[]{:S(2)}) collective-permute-start(bf16[128,24576]{0,1:T(8,128)(2,1)} %fusion.7), channel_id=1, source_target_pairs={{0,16},{1,17},{2,18},{3,19},{4,20},{5,21},{6,22},{7,23},{8,24},{9,... | collective-permute-start | bytes 18874376 | tf_op jit(solution)/shard_map/ppermute | solution.py:133
  1351.8 53.1 %collective-permute-start.116 = (bf16[256,2048]{1,0:T(8,128)(2,1)}, bf16[256,2048]{1,0:T(8,128)(2,1)S(1)}, u32[]{:S(2)}, u32[]{:S(2)}) collective-permute-start(bf16[256,2048]{1,0:T(8,128)(2,1)} %get-tuple-element.69), channel_id=1, source_target_pairs={{0,2},{1,3},{2,0},{3,1},{4,6},{5,7},{6,4},{7,5},{8,10},{9,11},{10,... | collective-permute-start | bytes 3145736 | tf_op jit(solution)/shard_map/ppermute | solution.py:129
  1353.6 49.1 %collective-permute-start.118 = (bf16[256,2048]{1,0:T(8,128)(2,1)}, bf16[256,2048]{1,0:T(8,128)(2,1)S(1)}, u32[]{:S(2)}, u32[]{:S(2)}) collective-permute-start(bf16[256,2048]{1,0:T(8,128)(2,1)} %get-tuple-element.69), channel_id=1, source_target_pairs={{0,4},{1,5},{2,6},{3,7},{4,0},{5,1},{6,2},{7,3},{8,12},{9,13},{10,... | collective-permute-start | bytes 3145736 | tf_op jit(solution)/shard_map/ppermute | solution.py:129
  1402.7 120.4 %collective-permute-start.115 = (bf16[256,2048]{1,0:T(8,128)(2,1)}, bf16[256,2048]{1,0:T(8,128)(2,1)S(1)}, u32[]{:S(2)}, u32[]{:S(2)}) collective-permute-start(bf16[256,2048]{1,0:T(8,128)(2,1)} %get-tuple-element.69), channel_id=1, source_target_pairs={{0,1},{1,0},{2,3},{3,2},{4,5},{5,4},{6,7},{7,6},{8,9},{9,8},{10,11... | collective-permute-start | bytes 3145736 | tf_op jit(solution)/shard_map/ppermute | solution.py:129
  1403.5 121.7 %collective-permute-start.120 = (bf16[128,2048]{1,0:T(8,128)(2,1)}, bf16[128,2048]{1,0:T(8,128)(2,1)}, u32[]{:S(2)}, u32[]{:S(2)}) collective-permute-start(bf16[128,2048]{1,0:T(8,128)(2,1)} %slice.356), channel_id=1, source_target_pairs={{0,2},{1,3},{2,0},{3,1},{4,6},{5,7},{6,4},{7,5},{8,10},{9,11},{10,... | collective-permute-start | bytes 1572872 | tf_op jit(solution)/shard_map/ppermute | solution.py:129
  1405.7 120.6 %collective-permute-start.121 = (bf16[128,2048]{1,0:T(8,128)(2,1)}, bf16[128,2048]{1,0:T(8,128)(2,1)}, u32[]{:S(2)}, u32[]{:S(2)}) collective-permute-start(bf16[128,2048]{1,0:T(8,128)(2,1)} %slice.357), channel_id=1, source_target_pairs={{0,4},{1,5},{2,6},{3,7},{4,0},{5,1},{6,2},{7,3},{8,12},{9,13},{10,... | collective-permute-start | bytes 1572872 | tf_op jit(solution)/shard_map/ppermute | solution.py:129
  1579.5 121.5 %collective-permute-start.123 = (bf16[4,256,2048]{2,1,0:T(8,128)(2,1)}, bf16[4,256,2048]{2,1,0:T(8,128)(2,1)}, u32[]{:S(2)}, u32[]{:S(2)}) collective-permute-start(bf16[4,256,2048]{2,1,0:T(8,128)(2,1)} %slice.291), channel_id=1, source_target_pairs={{0,1},{1,0},{2,3},{3,2},{4,5},{5,4},{6,7},{7,6},{8,9},{9,8},{10,11... | collective-permute-start | bytes 12582920 | tf_op jit(solution)/shard_map/ppermute | solution.py:129
  1579.8 37.5 %collective-permute-start.132 = (bf16[128,1024]{0,1:T(8,128)(2,1)S(1)}, bf16[128,1024]{0,1:T(8,128)(2,1)S(1)}, u32[]{:S(2)}, u32[]{:S(2)}) collective-permute-start(bf16[128,1024]{0,1:T(8,128)(2,1)S(1)} %get-tuple-element.147), channel_id=1, source_target_pairs={{0,10},{1,11},{2,8},{3,9},{4,14},{5,15},{6,12},{7,13},{8,2},{9,3},... | collective-permute-start | bytes 786440 | tf_op jit(solution)/shard_map/ppermute | solution.py:129
  1693.7 46.6 %collective-permute-start.143 = (bf16[128,8192]{1,0:T(8,128)(2,1)}, bf16[128,8192]{1,0:T(8,128)(2,1)}, u32[]{:S(2)}, u32[]{:S(2)}) collective-permute-start(bf16[128,8192]{1,0:T(8,128)(2,1)} %fusion.19), channel_id=1, source_target_pairs={{0,16},{1,17},{2,18},{3,19},{4,20},{5,21},{6,22},{7,23},{8,24},{9,... | collective-permute-start | bytes 6291464 | tf_op jit(solution)/shard_map/ppermute | solution.py:133
  (240 other events, 5626.9 us)
